TPU v7x, 256 devices: a whole 4x4x8 slice. The times are simulated.
256 devices in a mesh: grp: 4 (over y), row: 64 (over x, z, core).
Axes of the slice: x: 4, y: 4, z: 8, core: 2. Of those that a mesh axis runs over, the one named last changes fastest.
Arguments:
- embeddings: bfloat16 [65536, 4096], P(('grp', 'row')), may hold values from -200 to 200
- sketch: bfloat16 [4096, 128], replicated, may hold values from -6 to 6
Outputs:
- basis: float32 [65536, 128], P(('grp', 'row'))
- projected: float32 [4096, 128], replicated
All inputs are finite; a program needn't handle non-finite values.
Results may differ from a plain program's by a relative error of at most 0.0043.
Values may be sent and summed in bfloat16 or wider, within the bound.
A program may use at most 64 MiB of HBM per device.

v0:
```python
import math

import jax
import jax.numpy as jnp
from jax import lax
from jax.sharding import PartitionSpec as P

ITERS = 2


def inverse_factor(gram):
    lower = jnp.linalg.cholesky(gram)
    eye = jnp.eye(gram.shape[0], dtype=gram.dtype)
    return lax.linalg.triangular_solve(lower, eye, left_side=True, lower=True)


def gram_of(matrix):
    return jnp.dot(matrix.T, matrix, precision=lax.Precision.HIGHEST)


def apply_inverse(matrix, gram):
    return jnp.dot(matrix, inverse_factor(gram).T, precision=lax.Precision.HIGHEST)


def per_device(embeddings, sketch):
    devices = lax.axis_size("grp") * lax.axis_size("row")
    total = embeddings.shape[0] * devices
    scale = math.sqrt(total)

    def tall_basis(tall):
        gram = lax.psum(gram_of(tall), ("grp", "row"))
        return apply_inverse(tall, gram)

    def side_sum(q_low):
        local = lax.dot_general(
            embeddings, q_low, (((0,), (0,)), ((), ())), preferred_element_type=jnp.float32
        )
        return lax.psum(local, ("grp", "row"))

    tall = jnp.dot(embeddings, sketch, preferred_element_type=jnp.float32)
    current = tall_basis(tall)
    for step in range(ITERS):
        side = side_sum(current.astype(jnp.bfloat16))
        side_low = apply_inverse(side, gram_of(side)).astype(jnp.bfloat16)
        tall = jnp.dot(embeddings, side_low, preferred_element_type=jnp.float32)
        current = tall_basis(tall)
    final_side = side_sum(current.astype(jnp.bfloat16)) / scale
    return (current * scale, final_side)


def solution(mesh):
    placed = (P(("grp", "row"), None), P())
    return jax.shard_map(
        per_device,
        mesh=mesh,
        in_specs=placed,
        out_specs=(P(("grp", "row"), None), P()),
        check_vma=False,
    )
```

profile of v0, /device:TPU:1, one launch (start us, length us, event | category | flops | bytes accessed | tf_op | source)
XLA Modules:
  0.0 1663.9 jit_solution(12134692767255756427)
XLA Ops:
  7.2 0.0 all-reduce.7.cloned.1.call-start
  7.2 1.5 copy-done
  8.8 1.9 fusion.26
  10.7 1.0 fusion.27
  11.7 0.0 all-reduce.9.cloned.1.call-start
  11.8 244.2 %all-reduce.7.cloned.1.call-done = f32[128,128]{0,1:T(8,128)} async-done(((f32[128,128]{0,1:T(8,128)}), f32[128,128]{0,1:T(8,128)}) %all-reduce.7.cloned.1.call-update) | async-done | bytes 65552 | tf_op jit(solution)/shard_map/psum | solution.py:31
  256.0 0.9 copy.5
  256.9 0.9 fusion.24
  257.8 11.7 cholesky.89
  269.5 0.6 compare_reduce_fusion.4
  270.2 0.7 fusion.10
  270.8 9.8 custom-call.9
  280.6 0.3 fusion.8
  280.9 0.3 convolution_convert_fusion.3
  281.2 1.8 convolution_bitcast_fusion.2
  283.0 0.2 all-reduce.11.cloned.1.call-start
  283.3 255.7 %all-reduce.9.cloned.1.call-done = f32[4096,128]{0,1:T(8,128)} async-done(((f32[4096,128]{0,1:T(8,128)}), f32[4096,128]{0,1:T(8,128)}) %all-reduce.9.cloned.1.call-update) | async-done | bytes 2097168 | tf_op jit(solution)/shard_map/psum | solution.py:38
  538.9 4.0 fusion.28
  543.0 0.1 copy.6
  543.1 11.7 cholesky.100
  554.8 0.6 compare_reduce_fusion.3
  555.5 0.7 fusion.11
  556.2 9.8 custom-call.10
  566.0 0.3 fusion.6
  566.3 5.0 convolution_convert_fusion.1
  571.3 0.8 fusion.29
  572.1 1.1 fusion.30
  573.3 0.0 all-reduce.13.cloned.1.call-start
  573.3 238.2 %all-reduce.11.cloned.1.call-done = f32[128,128]{0,1:T(8,128)} async-done(((f32[128,128]{0,1:T(8,128)}), f32[128,128]{0,1:T(8,128)}) %all-reduce.11.cloned.1.call-update) | async-done | bytes 65552 | tf_op jit(solution)/shard_map/psum | solution.py:31
  811.6 0.9 copy.8
  812.5 0.9 fusion.20
  813.3 11.7 cholesky.111
  825.1 0.6 compare_reduce_fusion.2
  825.7 0.7 fusion.12
  826.4 9.8 custom-call.11
  836.2 0.3 fusion.4
  836.5 0.4 convolution_convert_fusion.2
  836.9 1.8 convolution_bitcast_fusion.1
  838.7 0.4 all-reduce.15.cloned.1.call-start
  839.2 255.4 %all-reduce.13.cloned.1.call-done = f32[4096,128]{0,1:T(8,128)} async-done(((f32[4096,128]{0,1:T(8,128)}), f32[4096,128]{0,1:T(8,128)}) %all-reduce.13.cloned.1.call-update) | async-done | bytes 2097168 | tf_op jit(solution)/shard_map/psum | solution.py:38
  1094.6 4.0 fusion.31
  1098.6 0.1 copy.9
  1098.8 11.7 cholesky.122
  1110.5 0.6 compare_reduce_fusion.1
  1111.2 0.7 fusion.13
  1111.8 9.8 custom-call.12
  1121.6 0.3 fusion.2
  1121.9 5.0 convolution_convert_fusion
  1127.0 0.8 fusion.32
  1127.8 1.1 fusion.33
  1128.9 0.0 all-reduce.17.cloned.1.call-start
  1129.0 238.2 %all-reduce.15.cloned.1.call-done = f32[128,128]{0,1:T(8,128)} async-done(((f32[128,128]{0,1:T(8,128)}), f32[128,128]{0,1:T(8,128)}) %all-reduce.15.cloned.1.call-update) | async-done | bytes 65552 | tf_op jit(solution)/shard_map/psum | solution.py:31
  1367.2 0.9 copy.11
  1368.1 0.9 fusion.16
  1368.9 11.7 cholesky.133
  1380.7 0.6 compare_reduce_fusion
  1381.3 0.7 fusion.14
  1382.0 9.8 custom-call.13
  1391.8 0.3 fusion
  1392.1 1.0 broadcast_multiply_fusion.1
  1393.2 1.8 convolution_bitcast_fusion
  1395.0 256.0 %all-reduce.17.cloned.1.call-done = f32[4096,128]{0,1:T(8,128)} async-done(((f32[4096,128]{0,1:T(8,128)}), f32[4096,128]{0,1:T(8,128)}) %all-reduce.17.cloned.1.call-update) | async-done | bytes 2097168 | tf_op jit(solution)/shard_map/psum | solution.py:38
  1650.9 3.1 broadcast_multiply_fusion
  1654.0 2.9 copy.12
  (14 shorter events, 0.3 us)
Async XLA Ops:
  7.2 1.6 copy-start
  7.2 248.8 %all-reduce.7.cloned.1.call-start = ((), (), s32[]{:S(2)}) async-start(), calls=%async_computation | async-start | bytes 131072 | tf_op jit(solution)/shard_map/psum | solution.py:31
  11.7 527.2 %all-reduce.9.cloned.1.call-start = ((), (), s32[]{:S(2)}) async-start(), calls=%async_computation.1 | async-start | bytes 4194304 | tf_op jit(solution)/shard_map/psum | solution.py:38
  283.0 528.5 %all-reduce.11.cloned.1.call-start = ((), (), s32[]{:S(2)}) async-start(), calls=%async_computation.2 | async-start | bytes 131072 | tf_op jit(solution)/shard_map/psum | solution.py:31
  573.3 521.3 %all-reduce.13.cloned.1.call-start = ((), (), s32[]{:S(2)}) async-start(), calls=%async_computation.3 | async-start | bytes 4194304 | tf_op jit(solution)/shard_map/psum | solution.py:38
  838.7 528.4 %all-reduce.15.cloned.1.call-start = ((), (), s32[]{:S(2)}) async-start(), calls=%async_computation.4 | async-start | bytes 131072 | tf_op jit(solution)/shard_map/psum | solution.py:31
  1128.9 522.0 %all-reduce.17.cloned.1.call-start = ((), (), s32[]{:S(2)}) async-start(), calls=%async_computation.5 | async-start | bytes 4194304 | tf_op jit(solution)/shard_map/psum | solution.py:38
Sparse Core Ops, SparseCore 0:
  14.1 241.8 all-reduce.6
  283.2 255.7 all-reduce.8
  573.4 238.0 all-reduce.10
  838.8 255.7 all-reduce.12
  1129.0 238.0 all-reduce.14
  1395.1 255.7 all-reduce.16
where the time goes:
time: 1670 us; the launch traced here: 1660 us
  waiting for transfers between devices  1490 us (89%)
  other arithmetic  120 us (7%)
  matrix products  33.5 us (2%)
    psum x3, waiting for transfers between devices, side_sum(): return lax.psum(local, ('grp', 'row'))  767 us
    psum x3, waiting for transfers between devices, tall_basis(): gram = lax.psum(gram_of(tall), ('grp', 'row'))  721 us
    another operation x15, other arithmetic, inverse_factor(): lower = jnp.linalg.cholesky(gram)  61.9 us
    another operation x10, other arithmetic, inverse_factor(): return lax.linalg.triangular_solve(lower, eye, left_side=True, lower=True)  52.3 us
  transfers between devices with their start and end apart: 6, of which 6 were waited for; matrix products, arithmetic and copies ran while one was open for 0% of the time, Pallas kernels for 0%

commit v1 on v0

v1 whole, which is shorter than its diff:
```python
import functools
import math

import jax
import jax.numpy as jnp
from jax import lax
from jax.experimental import pallas as pl
from jax.experimental.pallas import tpu as pltpu
from jax.sharding import PartitionSpec as P

ITERS = 2
STEPS = ITERS + 1
K = 128
D = 4096
HALF = D // 2
ROWS = 256
NX, NY, NZ, NC = 4, 4, 8, 2
PLANE = NX * NY
PIECE = K // NZ
F32 = jnp.float32
BF16 = jnp.bfloat16
MESH = pl.DeviceIdType.MESH
PLANE_STEPS = [(a, b) for a in range(NX) for b in range(NY) if (a, b) != (0, 0)]
NT = (((1,), (1,)), ((), ()))


def exact_dot(a, b, dims=(((1,), (0,)), ((), ()))):
    return lax.dot_general(
        a, b, dims, precision=lax.Precision.HIGHEST, preferred_element_type=F32
    )


def halves(value):
    high = value.astype(BF16)
    low = (value - high.astype(F32)).astype(BF16)
    return high, low


def lane_copy(value, j):
    index = jnp.full(value.shape, j, jnp.int32)
    return jnp.take_along_axis(value, index, axis=1)


def row_copy(value, j):
    return jnp.broadcast_to(value[j : j + 1, :], value.shape)


def inverse_factor(gram, out_ref):
    sub = lax.broadcasted_iota(jnp.int32, (8, K), 0)
    lane = lax.broadcasted_iota(jnp.int32, (8, K), 1)
    blocks = K // 8
    g = [gram[i] for i in range(blocks)]
    y = [jnp.where(lane == sub + 8 * i, 1.0, 0.0).astype(F32) for i in range(blocks)]
    for b in range(blocks):
        columns = [lane_copy(g[b], 8 * b + j) for j in range(8)]
        upper, inverse, g_rows, y_rows = {}, [], [], []
        scale = jnp.zeros((8, K), F32)
        for j in range(8):
            pivot = row_copy(columns[j], j)
            inverse.append(1.0 / pivot)
            scale = jnp.where(sub == j, lax.rsqrt(pivot), scale)
            factor = jnp.where(sub > j, columns[j] * inverse[j], 0.0)
            g_rows.append(row_copy(g[b], j))
            y_rows.append(row_copy(y[b], j))
            for m in range(j + 1, 8):
                upper[j, m] = row_copy(columns[m], j)
                columns[m] = columns[m] - factor * upper[j, m]
            g[b] = g[b] - factor * g_rows[j]
            y[b] = y[b] - factor * y_rows[j]
        for i in range(b + 1, blocks):
            factors = []
            gi, yi = g[i], y[i]
            for j in range(8):
                column = lane_copy(g[i], 8 * b + j)
                for m in range(j):
                    column = column - factors[m] * upper[m, j]
                factors.append(column * inverse[j])
                gi = gi - factors[j] * g_rows[j]
                yi = yi - factors[j] * y_rows[j]
            g[i], y[i] = gi, yi
        out_ref[8 * b : 8 * b + 8, :] = y[b] * scale


def kernel(
    a_hbm, s_hbm, side_out, t_out, y_out,
    a_tile, a_rest, s_all, t_ref, part, plane_in, block, z_in, side, gram_part,
    gram_in, gram_z, gram, y_t, y_s, side_n, sg_own, sg_in, tp_own, tp_in,
    local_sem, a_sem, t0_sem, rp_s, rp_r, rz_s, rz_r, az_s, az_r, ap_s, ap_r,
    gp_s, gp_r, gz_s, gz_r, ga_s, ga_r, sg_s, sg_r, tp_s, tp_r, fo_s, fo_r, fo_l,
):
    y = lax.axis_index("grp")
    row = lax.axis_index("row")
    x, z, core = row // (NZ * NC), (row // NC) % NZ, row % NC
    other = 1 - core
    here = x * NY + y

    def at(x_to, y_to, z_to, core_to):
        return (y_to, (x_to * NZ + z_to) * NC + core_to)

    def plane_peer(step):
        x_to, y_to = (x + step[0]) % NX, (y + step[1]) % NY
        return x_to * NY + y_to, at(x_to, y_to, z, core)

    def z_peer(step):
        z_to = (z + step) % NZ
        return z_to, at(x, y, z_to, core)

    partner = at(x, y, z, other)
    plane_peers = [plane_peer(step) for step in PLANE_STEPS]
    z_peers = [z_peer(step) for step in range(1, NZ)]

    def send(src, dst, send_sem, recv_sem, device):
        return pltpu.make_async_remote_copy(
            src, dst, send_sem, recv_sem, device_id=device, device_id_type=MESH
        )

    own_half = pl.ds(pl.multiple_of(core * HALF, HALF), HALF)
    other_half = pl.ds(pl.multiple_of(other * HALF, HALF), HALF)
    loads = [
        pltpu.make_async_copy(a_hbm.at[:, own_half], a_tile.at[core], local_sem.at[0]),
        pltpu.make_async_copy(a_hbm.at[:, other_half], a_rest, local_sem.at[1]),
        pltpu.make_async_copy(s_hbm, s_all, local_sem.at[2]),
    ]
    for copy in loads:
        copy.start()

    barrier = pltpu.get_barrier_semaphore()
    everyone = [device for _, device in plane_peers + z_peers] + [partner]
    for device in everyone:
        pl.semaphore_signal(barrier, inc=1, device_id=device, device_id_type=MESH)
    pl.semaphore_wait(barrier, len(everyone))

    swap_a = send(
        a_hbm.at[:, other_half], a_tile.at[core], a_sem.at[0], a_sem.at[1], partner
    )
    swap_a.start()
    for copy in loads:
        copy.wait()
    first = jnp.dot(a_tile[core], s_all[own_half, :], preferred_element_type=F32)
    first = first + jnp.dot(a_rest[...], s_all[other_half, :], preferred_element_type=F32)
    t_ref[core] = first.T
    swap_t = send(t_ref.at[core], t_ref.at[core], t0_sem.at[0], t0_sem.at[1], partner)
    swap_t.start()
    swap_t.wait()
    swap_a.wait()

    def step_body(k, carry):
        t0, t1 = t_ref[0], t_ref[1]
        local = exact_dot(t0, t0, NT) + exact_dot(t1, t1, NT)
        for i in range(PLANE):
            gram_part[i] = local[8 * i : 8 * i + 8, :]
        sends = []
        gram_copies = []
        for i, (q, device) in enumerate(plane_peers):
            copy = send(gram_part.at[q], gram_in.at[k, i], gp_s.at[i], gp_r.at[k, i], device)
            copy.start()
            gram_copies.append(copy)

        h0, l0 = halves(t0)
        h1, l1 = halves(t1)
        t0_split = jnp.concatenate([h0, l0], axis=0)
        t1_split = jnp.concatenate([h1, l1], axis=0)
        for j in range(PLANE // 2):
            columns = slice(2 * K * j, 2 * K * (j + 1))
            value = jnp.dot(t0_split, a_tile[0, :, columns], preferred_element_type=F32)
            value = value + jnp.dot(t1_split, a_tile[1, :, columns], preferred_element_type=F32)
            value = value[:K] + value[K:]
            part[2 * j] = value[:, :K]
            part[2 * j + 1] = value[:, K:]
        side_copies = []
        for i, (q, device) in enumerate(plane_peers):
            copy = send(part.at[q], plane_in.at[k, i], rp_s.at[i], rp_r.at[k, i], device)
            copy.start()
            side_copies.append(copy)

        value = gram_part[here]
        for i, copy in enumerate(gram_copies):
            copy.wait_recv()
            value = value + gram_in[k, i]
        gram_z[k, z] = value
        gram_z_copies = []
        for i, (_, device) in enumerate(z_peers):
            copy = send(gram_z.at[k, z], gram_z.at[k, z], gz_s.at[i], gz_r.at[k, i], device)
            copy.start()
            gram_z_copies.append(copy)

        value = part[here]
        for i, copy in enumerate(side_copies):
            copy.wait_recv()
            value = value + plane_in[k, i]
        for i in range(NZ):
            block[i] = value[PIECE * i : PIECE * (i + 1), :]
        z_copies = []
        for i, (q, device) in enumerate(z_peers):
            copy = send(block.at[q], z_in.at[k, i], rz_s.at[i], rz_r.at[k, i], device)
            copy.start()
            z_copies.append(copy)

        for copy in gram_z_copies:
            copy.wait_recv()
        value = gram_z[k, 0]
        for i in range(1, NZ):
            value = value + gram_z[k, i]
        gram[k, here] = value
        gram_all_copies = []
        for i, (_, device) in enumerate(plane_peers):
            copy = send(gram.at[k, here], gram.at[k, here], ga_s.at[i], ga_r.at[k, i], device)
            copy.start()
            gram_all_copies.append(copy)

        value = block[z]
        for i, copy in enumerate(z_copies):
            copy.wait_recv()
            value = value + z_in[k, i]
        side[k, here, z] = value
        z_all_copies = []
        for i, (_, device) in enumerate(z_peers):
            copy = send(
                side.at[k, here, z], side.at[k, here, z], az_s.at[i], az_r.at[k, i], device
            )
            copy.start()
            z_all_copies.append(copy)

        for copy in gram_all_copies:
            copy.wait_recv()
        inverse_factor([gram[k, i] for i in range(PLANE)], y_t)

        for copy in z_all_copies:
            copy.wait_recv()
        all_copies = []
        for i, (_, device) in enumerate(plane_peers):
            copy = send(side.at[k, here], side.at[k, here], ap_s.at[i], ap_r.at[k, i], device)
            copy.start()
            all_copies.append(copy)
        for copy in all_copies:
            copy.wait_recv()
        for copy in (
            gram_copies + side_copies + gram_z_copies + z_copies
            + gram_all_copies + z_all_copies + all_copies
        ):
            copy.wait_send()

        @pl.when(k < ITERS)
        def _():
            y_value = y_t[...]
            total = jnp.zeros((K, K), F32)
            for j in range(PLANE // 2):
                pair = jnp.concatenate(
                    [side[k, 2 * j].reshape(K, K), side[k, 2 * j + 1].reshape(K, K)], axis=1
                )
                value = exact_dot(y_value, pair)
                total = total + exact_dot(value, value, NT)
                side_n[:, 2 * K * j : 2 * K * (j + 1)] = value
            sg_own[...] = total
            swap_gram = send(sg_own, sg_in.at[k], sg_s.at[0], sg_r.at[k], partner)
            swap_gram.start()
            high, low = halves(side_n[...])
            split = jnp.concatenate([high, low], axis=0)
            for half in range(NC):
                value = lax.dot_general(split, a_tile[half], NT, preferred_element_type=F32)
                tp_own[half] = value[:K] + value[K:]
            swap_part = send(tp_own, tp_in.at[k], tp_s.at[0], tp_r.at[k], partner)
            swap_part.start()
            swap_gram.wait()
            total = sg_own[...] + sg_in[k]
            inverse_factor([total[8 * i : 8 * i + 8, :] for i in range(PLANE)], y_s)
            swap_part.wait()
            y_value = y_s[...]
            for half in range(NC):
                t_ref[half] = exact_dot(y_value, tp_own[half] + tp_in[k, half])

        return carry

    lax.fori_loop(0, STEPS, step_body, 0)

    last = STEPS - 1
    outs = []
    for i in range(PLANE):
        keep = pltpu.make_async_copy(side.at[last, i], side_out.at[core, i], fo_l.at[i])
        give = send(side.at[last, i], side_out.at[core, i], fo_s.at[i], fo_r.at[i], partner)
        keep.start()
        give.start()
        outs += [keep, give]
    t_out[...] = t_ref[core]
    y_out[...] = y_t[...]
    for copy in outs:
        copy.wait()


def sweep(embeddings, sketch):
    vmem = pl.BlockSpec(memory_space=pltpu.VMEM)
    hbm = pl.BlockSpec(memory_space=pl.ANY)
    dma = pltpu.SemaphoreType.DMA
    near, far = PLANE - 1, NZ - 1
    return pl.pallas_call(
        kernel,
        out_shape=(
            jax.ShapeDtypeStruct((NC, PLANE, NZ, PIECE, K), F32),
            jax.ShapeDtypeStruct((K, ROWS), F32),
            jax.ShapeDtypeStruct((K, K), F32),
        ),
        in_specs=[hbm, hbm],
        out_specs=(hbm, vmem, vmem),
        scratch_shapes=[
            pltpu.VMEM((NC, ROWS, HALF), BF16),
            pltpu.VMEM((ROWS, HALF), BF16),
            pltpu.VMEM((D, K), BF16),
            pltpu.VMEM((NC, K, ROWS), F32),
            pltpu.VMEM((PLANE, K, K), F32),
            pltpu.VMEM((STEPS, near, K, K), F32),
            pltpu.VMEM((NZ, PIECE, K), F32),
            pltpu.VMEM((STEPS, far, PIECE, K), F32),
            pltpu.VMEM((STEPS, PLANE, NZ, PIECE, K), F32),
            pltpu.VMEM((PLANE, 8, K), F32),
            pltpu.VMEM((STEPS, near, 8, K), F32),
            pltpu.VMEM((STEPS, NZ, 8, K), F32),
            pltpu.VMEM((STEPS, PLANE, 8, K), F32),
            pltpu.VMEM((K, K), F32),
            pltpu.VMEM((K, K), F32),
            pltpu.VMEM((K, HALF), F32),
            pltpu.VMEM((K, K), F32),
            pltpu.VMEM((ITERS, K, K), F32),
            pltpu.VMEM((NC, K, ROWS), F32),
            pltpu.VMEM((ITERS, NC, K, ROWS), F32),
            dma((3,)), dma((2,)), dma((2,)),
            dma((near,)), dma((STEPS, near)),
            dma((far,)), dma((STEPS, far)),
            dma((far,)), dma((STEPS, far)),
            dma((near,)), dma((STEPS, near)),
            dma((near,)), dma((STEPS, near)),
            dma((far,)), dma((STEPS, far)),
            dma((near,)), dma((STEPS, near)),
            dma((1,)), dma((ITERS,)),
            dma((1,)), dma((ITERS,)),
            dma((PLANE,)), dma((PLANE,)), dma((PLANE,)),
        ],
        compiler_params=pltpu.CompilerParams(
            collective_id=0, has_side_effects=True, vmem_limit_bytes=40 * 2**20
        ),
        name="sweep",
    )(embeddings, sketch)


def per_device(embeddings, sketch):
    devices = lax.axis_size("grp") * lax.axis_size("row")
    scale = math.sqrt(embeddings.shape[0] * devices)
    side, t, inverse = sweep(embeddings, sketch)
    side = side.reshape(NC * PLANE, K, K)
    basis = exact_dot(t, inverse * scale, (((0,), (1,)), ((), ())))
    projected = exact_dot(side, inverse / scale, (((1,), (1,)), ((), ())))
    return basis, projected.reshape(D, K)


def solution(mesh):
    return jax.shard_map(
        per_device,
        mesh=mesh,
        in_specs=(P(("grp", "row"), None), P()),
        out_specs=(P(("grp", "row"), None), P()),
        check_vma=False,
    )
```

time: 1670 us -> 172 us (0.10)
  waiting for transfers between devices: 1490 us -> 0 us
  Pallas kernels: 0 us -> 160 us
  other arithmetic: 120 us -> 0 us
  matrix products: 33.5 us -> 5.76 us
    psum x6 -> x0, waiting for transfers between devices: 1490 us -> none  [the longest x3 767 us: side_sum(): return lax.psum(local, ('grp', 'row'))]
    pallas_call x0 -> x1, Pallas kernels: none -> 160 us  [sweep(): pl.pallas_call(kernel, out_shape=(jax.ShapeDtypeStruct((NC, PLANE, NZ, PI...]
    another operation x25 -> x0, other arithmetic: 114 us -> none  [the longest x15 61.9 us: inverse_factor(): lower = jnp.linalg.cholesky(gram)]
    dot_general x16 -> x2, matrix products: 32 us -> 5.76 us  [exact_dot(): lax.dot_general(a, b, dims, precision=lax.Precision.HIGHEST, preferred_el...]
  transfers between devices with their start and end apart: 6 -> 0, of which waited for: 6 -> 0; matrix products, arithmetic and copies ran while one was open for 0% -> 0% of each run, Pallas kernels for 0% -> 0%
where the time goes in v1:
time: 172 us; the launch traced here: 171 us
  Pallas kernels  160 us (93%)
  matrix products  5.76 us (3%)
  local copies, waits for them, and re-layouts  4.66 us (3%)
    pallas_call x1, Pallas kernels, sweep(): pl.pallas_call(kernel, out_shape=(jax.ShapeDtypeStruct((NC, PLANE, NZ, PI...  160 us
    dot_general x2, matrix products, exact_dot(): lax.dot_general(a, b, dims, precision=lax.Precision.HIGHEST, preferred_el...  5.76 us

profile of v1, /device:TPU:1, one launch (start us, length us, event | category | flops | bytes accessed | tf_op | source)
XLA Modules:
  0.0 171.4 jit_solution(3937689078698425746)
XLA Ops:
  0.6 0.0 copy-start
  0.6 1.6 copy-done
  2.2 0.0 copy-start.1
  2.2 1.2 copy-done.1
  3.4 160.4 %sweep.1 = (f32[2,16,8,16,128]{4,3,2,1,0:T(8,128)S(1)}, f32[128,256]{1,0:T(8,128)S(1)}, f32[128,128]{1,0:T(8,128)S(1)}) custom-call(bf16[256,4096]{1,0:T(8,128)(2,1)S(1)} %copy-done, bf16[4096,128]{1,0:T(8,128)(2,1)S(1)} %copy-done.1), custom_call_target="tpu_custom_call" | custom-call | tf_op jit(solution)/shard_map/sweep/pallas_call | solution.py:295
  163.8 1.0 fusion.2
  164.9 1.9 %copy.4 = f32[32,128,128]{1,2,0:T(8,128)} copy(f32[32,128,128]{2,1,0:T(8,128)S(1)} %bitcast.6) | data formatting | bytes 4194304 | tf_op jit(solution)/shard_map/reshape | solution.py:348
  166.7 4.7 %fusion = f32[4096,128]{1,0:T(8,128)} fusion(f32[4096,128]{1,0:T(8,128)} %bitcast.7, f32[128,128]{1,0:T(8,128)S(1)} %get-tuple-element.6), kind=kOutput, calls=%fused_computation | convolution fusion | flops 805322752 | bytes 4259840 | tf_op jit(solution)/shard_map/dot_general | solution.py:28
Async XLA Ops:
  0.6 1.6 copy-start
  2.2 1.2 copy-start.1

commit v2 on v1

v2 whole, which is shorter than its diff:
```python
import functools
import math

import jax
import jax.numpy as jnp
from jax import lax
from jax.experimental import pallas as pl
from jax.experimental.pallas import tpu as pltpu
from jax.sharding import PartitionSpec as P

ITERS = 2
STEPS = ITERS + 1
K = 128
D = 4096
HALF = D // 2
ROWS = 256
NX, NY, NZ, NC = 4, 4, 8, 2
PLANE = NX * NY
PIECE = K // NZ
F32 = jnp.float32
BF16 = jnp.bfloat16
MESH = pl.DeviceIdType.MESH
PLANE_STEPS = [(a, b) for a in range(NX) for b in range(NY) if (a, b) != (0, 0)]
Z_STEPS = list(range(1, NZ))
SCALE = math.sqrt(ROWS * NX * NY * NZ * NC)
NT = (((1,), (1,)), ((), ()))


def exact_dot(a, b, dims=(((1,), (0,)), ((), ()))):
    return lax.dot_general(
        a, b, dims, precision=lax.Precision.HIGHEST, preferred_element_type=F32
    )


def halves(value):
    high = value.astype(BF16)
    low = (value - high.astype(F32)).astype(BF16)
    return high, low


def lane_copy(value, j):
    index = jnp.full(value.shape, j, jnp.int32)
    return jnp.take_along_axis(value, index, axis=1)


def row_copy(value, j):
    return jnp.broadcast_to(value[j : j + 1, :], value.shape)


def inverse_factor(gram, out_ref):
    sub = lax.broadcasted_iota(jnp.int32, (8, K), 0)
    lane = lax.broadcasted_iota(jnp.int32, (8, K), 1)
    blocks = K // 8
    g = [gram[i] for i in range(blocks)]
    y = [jnp.where(lane == sub + 8 * i, 1.0, 0.0).astype(F32) for i in range(blocks)]
    for b in range(blocks):
        columns = [lane_copy(g[b], 8 * b + j) for j in range(8)]
        upper, inverse, g_rows, y_rows = {}, [], [], []
        scale = jnp.zeros((8, K), F32)
        for j in range(8):
            pivot = row_copy(columns[j], j)
            inverse.append(1.0 / pivot)
            scale = jnp.where(sub == j, lax.rsqrt(pivot), scale)
            factor = jnp.where(sub > j, columns[j] * inverse[j], 0.0)
            g_rows.append(row_copy(g[b], j))
            y_rows.append(row_copy(y[b], j))
            for m in range(j + 1, 8):
                upper[j, m] = row_copy(columns[m], j)
                columns[m] = columns[m] - factor * upper[j, m]
            g[b] = g[b] - factor * g_rows[j]
            y[b] = y[b] - factor * y_rows[j]
        for i in range(b + 1, blocks):
            factors = []
            gi, yi = g[i], y[i]
            for j in range(8):
                column = lane_copy(g[i], 8 * b + j)
                for m in range(j):
                    column = column - factors[m] * upper[m, j]
                factors.append(column * inverse[j])
                gi = gi - factors[j] * g_rows[j]
                yi = yi - factors[j] * y_rows[j]
            g[i], y[i] = gi, yi
        out_ref[8 * b : 8 * b + 8, :] = y[b] * scale


def kernel(
    a_hbm, s_hbm, proj_out, basis_out,
    a_tile, a_rest, s_all, t_ref, part_wide, part_slim, in_wide, in_slim, block, z_in,
    z_all, side_wide, side_slim, gram_part, gram_in, gram_z, gram, y_t, y_s,
    sg_own, sg_in, tp_own, tp_in,
    local_sem, a_sem, t0_sem, rp_s, rp_r, rz_s, rz_r, az_s, az_r, ap_s, ap_r,
    gp_s, gp_r, gz_s, gz_r, ga_s, ga_r, sg_s, sg_r, tp_s, tp_r, fo_s, fo_r, fo_l,
):
    y = lax.axis_index("grp")
    row = lax.axis_index("row")
    x, z, core = row // (NZ * NC), (row // NC) % NZ, row % NC
    other = 1 - core
    here = x * NY + y

    def at(x_to, y_to, z_to, core_to):
        return (y_to, (x_to * NZ + z_to) * NC + core_to)

    def plane_peer(step):
        x_to, y_to = (x + step[0]) % NX, (y + step[1]) % NY
        return x_to * NY + y_to, at(x_to, y_to, z, core)

    def plane_source(i):
        x_from, y_from = (x - PLANE_STEPS[i][0]) % NX, (y - PLANE_STEPS[i][1]) % NY
        return x_from * NY + y_from

    def z_peer(step):
        z_to = (z + step) % NZ
        return z_to, at(x, y, z_to, core)

    partner = at(x, y, z, other)
    plane_peers = [plane_peer(step) for step in PLANE_STEPS]
    z_peers = [z_peer(step) for step in Z_STEPS]

    def send(src, dst, send_sem, recv_sem, device):
        copy = pltpu.make_async_remote_copy(
            src, dst, send_sem, recv_sem, device_id=device, device_id_type=MESH
        )
        copy.start()
        return copy

    own_half = pl.ds(pl.multiple_of(core * HALF, HALF), HALF)
    other_half = pl.ds(pl.multiple_of(other * HALF, HALF), HALF)
    loads = [
        pltpu.make_async_copy(a_hbm.at[:, own_half], a_tile.at[core], local_sem.at[0]),
        pltpu.make_async_copy(a_hbm.at[:, other_half], a_rest, local_sem.at[1]),
        pltpu.make_async_copy(s_hbm, s_all, local_sem.at[2]),
    ]
    for copy in loads:
        copy.start()

    barrier = pltpu.get_barrier_semaphore()
    everyone = [device for _, device in plane_peers + z_peers] + [partner]
    for device in everyone:
        pl.semaphore_signal(barrier, inc=1, device_id=device, device_id_type=MESH)
    for copy in loads:
        copy.wait()
    first = jnp.dot(a_tile[core], s_all[own_half, :], preferred_element_type=F32)
    first = first + jnp.dot(a_rest[...], s_all[other_half, :], preferred_element_type=F32)
    t_ref[core] = first.T
    pl.semaphore_wait(barrier, len(everyone))

    swap_t = send(t_ref.at[core], t_ref.at[core], t0_sem.at[0], t0_sem.at[1], partner)
    swap_a = send(a_rest, a_tile.at[core], a_sem.at[0], a_sem.at[1], partner)
    swap_t.wait()

    for k in range(STEPS):
        wide, last = k == 0, k == ITERS
        part, into, whole = (
            (part_wide, in_wide, side_wide)
            if wide
            else (part_slim, in_slim.at[k - 1], side_slim.at[k - 1])
        )
        travel = part.dtype

        t0, t1 = t_ref[0], t_ref[1]
        local = exact_dot(t0, t0, NT) + exact_dot(t1, t1, NT)
        for i in range(PLANE):
            gram_part[i] = local[8 * i : 8 * i + 8, :]
        gram_copies = [
            send(gram_part.at[q], gram_in.at[k, i], gp_s.at[i], gp_r.at[k, i], device)
            for i, (q, device) in enumerate(plane_peers)
        ]

        if wide:
            swap_a.wait()
        t0_split = jnp.concatenate(halves(t0), axis=0)
        t1_split = jnp.concatenate(halves(t1), axis=0)
        for j in range(PLANE // 2):
            columns = slice(2 * K * j, 2 * K * (j + 1))
            value = jnp.dot(t0_split, a_tile[0, :, columns], preferred_element_type=F32)
            value = value + jnp.dot(t1_split, a_tile[1, :, columns], preferred_element_type=F32)
            value = value[:K] + value[K:]
            part[2 * j] = value[:, :K].astype(travel)
            part[2 * j + 1] = value[:, K:].astype(travel)
        side_copies = [
            send(part.at[q], into.at[i], rp_s.at[i], rp_r.at[k, i], device)
            for i, (q, device) in enumerate(plane_peers)
        ]

        value = gram_part[here]
        for i, copy in enumerate(gram_copies):
            copy.wait_recv()
            value = value + gram_in[k, i]
        gram_z[k, z] = value
        gram_z_copies = [
            send(gram_z.at[k, z], gram_z.at[k, z], gz_s.at[i], gz_r.at[k, i], device)
            for i, (_, device) in enumerate(z_peers)
        ]

        value = part[here].astype(F32)
        for i, copy in enumerate(side_copies):
            copy.wait_recv()
            value = value + into[i].astype(F32)
        for i in range(NZ):
            block[i] = value[PIECE * i : PIECE * (i + 1), :]
        z_copies = [
            send(block.at[q], z_in.at[k, i], rz_s.at[i], rz_r.at[k, i], device)
            for i, (q, device) in enumerate(z_peers)
        ]

        for copy in gram_z_copies:
            copy.wait_recv()
        value = gram_z[k, 0]
        for i in range(1, NZ):
            value = value + gram_z[k, i]
        gram[k, here] = value
        gram_all_copies = [
            send(gram.at[k, here], gram.at[k, here], ga_s.at[i], ga_r.at[k, i], device)
            for i, (_, device) in enumerate(plane_peers)
        ]

        value = block[z]
        for i, copy in enumerate(z_copies):
            copy.wait_recv()
            value = value + z_in[k, i]
        z_all[k, z] = value
        z_all_copies = [
            send(z_all.at[k, z], z_all.at[k, z], az_s.at[i], az_r.at[k, i], device)
            for i, (_, device) in enumerate(z_peers)
        ]

        for copy in gram_all_copies:
            copy.wait_recv()
        inverse_factor([gram[k, i] for i in range(PLANE)], y_t)
        y_value = y_t[...]

        for copy in z_all_copies:
            copy.wait_recv()
        value = z_all[k].reshape(K, K)
        if last:
            value = exact_dot(value, y_value / SCALE, (((0,), (1,)), ((), ())))
        else:
            value = exact_dot(y_value, value)
        whole[here] = value.astype(travel)
        all_copies = [
            send(whole.at[here], whole.at[here], ap_s.at[i], ap_r.at[k, i], device)
            for i, (_, device) in enumerate(plane_peers)
        ]
        outs = []

        def pass_on(i, q):
            keep = pltpu.make_async_copy(whole.at[q], proj_out.at[core, q], fo_l.at[i])
            keep.start()
            give = send(whole.at[q], proj_out.at[core, q], fo_s.at[i], fo_r.at[i], partner)
            outs.extend([keep, give])

        if last:
            pass_on(PLANE - 1, here)
            basis_out[...] = exact_dot(
                t_ref[core], y_value * SCALE, (((0,), (1,)), ((), ()))
            )
        for i, copy in enumerate(all_copies):
            copy.wait_recv()
            if last:
                pass_on(i, plane_source(i))
        for copy in (
            gram_copies + side_copies + gram_z_copies + z_copies
            + gram_all_copies + z_all_copies + all_copies
        ):
            copy.wait_send()
        for copy in outs:
            copy.wait()
        if last:
            break

        pairs = []
        for j in range(PLANE // 2):
            pair = jnp.concatenate([whole[2 * j], whole[2 * j + 1]], axis=1)
            pairs.append(jnp.concatenate(halves(pair), axis=0) if wide else pair)
        split = jnp.concatenate(pairs, axis=1)
        total = lax.dot_general(split, split, NT, preferred_element_type=F32)
        if wide:
            total = total[:K] + total[K:]
            total = total[:, :K] + total[:, K:]
        sg_own[...] = total
        swap_gram = send(sg_own, sg_in.at[k], sg_s.at[0], sg_r.at[k], partner)
        for half in range(NC):
            value = lax.dot_general(split, a_tile[half], NT, preferred_element_type=F32)
            tp_own[half] = value[:K] + value[K:] if wide else value
        swap_part = send(tp_own, tp_in.at[k], tp_s.at[0], tp_r.at[k], partner)
        swap_gram.wait()
        total = sg_own[...] + sg_in[k]
        inverse_factor([total[8 * i : 8 * i + 8, :] for i in range(PLANE)], y_s)
        swap_part.wait()
        y_value = y_s[...]
        for half in range(NC):
            t_ref[half] = exact_dot(y_value, tp_own[half] + tp_in[k, half])


def sweep(embeddings, sketch):
    vmem = pl.BlockSpec(memory_space=pltpu.VMEM)
    hbm = pl.BlockSpec(memory_space=pl.ANY)
    dma = pltpu.SemaphoreType.DMA
    near, far = PLANE - 1, NZ - 1
    return pl.pallas_call(
        kernel,
        out_shape=(
            jax.ShapeDtypeStruct((NC, PLANE, K, K), BF16),
            jax.ShapeDtypeStruct((ROWS, K), F32),
        ),
        in_specs=[hbm, hbm],
        out_specs=(hbm, vmem),
        scratch_shapes=[
            pltpu.VMEM((NC, ROWS, HALF), BF16),
            pltpu.VMEM((ROWS, HALF), BF16),
            pltpu.VMEM((D, K), BF16),
            pltpu.VMEM((NC, K, ROWS), F32),
            pltpu.VMEM((PLANE, K, K), F32),
            pltpu.VMEM((PLANE, K, K), BF16),
            pltpu.VMEM((near, K, K), F32),
            pltpu.VMEM((ITERS, near, K, K), BF16),
            pltpu.VMEM((NZ, PIECE, K), F32),
            pltpu.VMEM((STEPS, far, PIECE, K), F32),
            pltpu.VMEM((STEPS, NZ, PIECE, K), F32),
            pltpu.VMEM((PLANE, K, K), F32),
            pltpu.VMEM((ITERS, PLANE, K, K), BF16),
            pltpu.VMEM((PLANE, 8, K), F32),
            pltpu.VMEM((STEPS, near, 8, K), F32),
            pltpu.VMEM((STEPS, NZ, 8, K), F32),
            pltpu.VMEM((STEPS, PLANE, 8, K), F32),
            pltpu.VMEM((K, K), F32),
            pltpu.VMEM((K, K), F32),
            pltpu.VMEM((K, K), F32),
            pltpu.VMEM((ITERS, K, K), F32),
            pltpu.VMEM((NC, K, ROWS), F32),
            pltpu.VMEM((ITERS, NC, K, ROWS), F32),
            dma((3,)), dma((2,)), dma((2,)),
            dma((near,)), dma((STEPS, near)),
            dma((far,)), dma((STEPS, far)),
            dma((far,)), dma((STEPS, far)),
            dma((near,)), dma((STEPS, near)),
            dma((near,)), dma((STEPS, near)),
            dma((far,)), dma((STEPS, far)),
            dma((near,)), dma((STEPS, near)),
            dma((1,)), dma((ITERS,)),
            dma((1,)), dma((ITERS,)),
            dma((PLANE,)), dma((PLANE,)), dma((PLANE,)),
        ],
        compiler_params=pltpu.CompilerParams(
            collective_id=0, has_side_effects=True, vmem_limit_bytes=62 * 2**20
        ),
        name="sweep",
    )(embeddings, sketch)


def per_device(embeddings, sketch):
    projected, basis = sweep(embeddings, sketch)
    return basis, projected.reshape(D, K).astype(F32)


def solution(mesh):
    return jax.shard_map(
        per_device,
        mesh=mesh,
        in_specs=(P(("grp", "row"), None), P()),
        out_specs=(P(("grp", "row"), None), P()),
        check_vma=False,
    )
```

time: 172 us -> 134 us (0.78)
  Pallas kernels: 160 us -> 130 us
  matrix products: 5.76 us -> 0 us
  local copies, waits for them, and re-layouts: 4.66 us -> 0.66 us
  other arithmetic: 0 us -> 2.71 us
    pallas_call x1, Pallas kernels: 160 us -> 130 us  [sweep(): pl.pallas_call(kernel, out_shape=(jax.ShapeDtypeStruct((NC, PLANE, K, K),...]
    dot_general x2 -> x0, matrix products: 5.76 us -> none  [exact_dot(): lax.dot_general(a, b, dims, precision=lax.Precision.HIGHEST, preferred_el...]
    convert_element_type x0 -> x1, other arithmetic: none -> 2.71 us  [per_device(): return (basis, projected.reshape(D, K).astype(F32))]
    unnamed x4 -> x3, local copies, waits for them, and re-layouts: 2.81 us -> 0.66 us
    reshape x1 -> x0, local copies, waits for them, and re-layouts: 1.85 us -> none  [per_device(): side = side.reshape(NC * PLANE, K, K)]
where the time goes in v2:
time: 134 us
  Pallas kernels  130 us (97%)
  other arithmetic  2.71 us (2%)
    pallas_call x1, Pallas kernels, sweep(): pl.pallas_call(kernel, out_shape=(jax.ShapeDtypeStruct((NC, PLANE, K, K),...  130 us
    convert_element_type x1, other arithmetic, per_device(): return (basis, projected.reshape(D, K).astype(F32))  2.71 us

profile of v2, /device:TPU:1, one launch (start us, length us, event | category | flops | bytes accessed | tf_op | source)
XLA Modules:
  0.0 134.1 jit_solution(9862641011916419507)
XLA Ops:
  0.6 130.1 %sweep.1 = (bf16[2,16,128,128]{3,2,1,0:T(8,128)(2,1)}, f32[256,128]{1,0:T(8,128)}) custom-call(bf16[256,4096]{1,0:T(8,128)(2,1)} %a_hbm.1, bf16[4096,128]{1,0:T(8,128)(2,1)} %s_hbm.1), custom_call_target="tpu_custom_call" | custom-call | tf_op jit(solution)/shard_map/sweep/pallas_call | solution.py:300
  130.8 0.0 copy-start
  130.8 2.7 %bitcast_convert_fusion = f32[4096,128]{1,0:T(8,128)} fusion(bf16[2,16,128,128]{3,2,1,0:T(8,128)(2,1)} %get-tuple-element.5), kind=kLoop, calls=%fused_computation | loop fusion | flops 524288 | bytes 3145728 | tf_op jit(solution)/shard_map/convert_element_type | solution.py:353
  133.5 0.0 copy-done
  133.5 0.7 copy.5
Async XLA Ops:
  130.8 2.7 %copy-start = (f32[256,128]{1,0:T(8,128)S(1)}, f32[256,128]{1,0:T(8,128)}, u32[]{:S(2)}) copy-start(f32[256,128]{1,0:T(8,128)} %get-tuple-element.8) | copy-start | bytes 393220

commit v3 on v2

v3 whole, which is shorter than its diff:
```python
import math

import jax
import jax.numpy as jnp
from jax import lax
from jax.experimental import pallas as pl
from jax.experimental.pallas import tpu as pltpu
from jax.sharding import PartitionSpec as P

ITERS = 2
STEPS = ITERS + 1
K = 128
D = 4096
HALF = D // 2
ROWS = 256
NX, NY, NZ, NC = 4, 4, 8, 2
PLANE = NX * NY
PIECE = K // NZ
F32 = jnp.float32
BF16 = jnp.bfloat16
MESH = pl.DeviceIdType.MESH


def hops(step, size):
    return min(step, size - step)


RING = [2, 1, 3]
Z_STEPS = sorted(range(1, NZ), key=lambda c: -hops(c, NZ))
PLANE_STEPS = sorted(
    [(a, b) for a in range(NX) for b in range(NY) if (a, b) != (0, 0)],
    key=lambda c: -hops(c[0], NX) - hops(c[1], NY),
)
SCALE = math.sqrt(ROWS * NX * NY * NZ * NC)
NT = (((1,), (1,)), ((), ()))
TN = (((0,), (1,)), ((), ()))
TOP, LOW = pl.ds(0, K // 2), pl.ds(K // 2, K // 2)


def exact_dot(a, b, dims=(((1,), (0,)), ((), ()))):
    return lax.dot_general(
        a, b, dims, precision=lax.Precision.HIGHEST, preferred_element_type=F32
    )


def halves(value):
    high = value.astype(BF16)
    low = (value - high.astype(F32)).astype(BF16)
    return high, low


def lane_copy(value, j):
    index = jnp.full(value.shape, j, jnp.int32)
    return jnp.take_along_axis(value, index, axis=1)


def row_copy(value, j):
    return jnp.broadcast_to(value[j : j + 1, :], value.shape)


def inverse_factor(gram, out_ref):
    sub = lax.broadcasted_iota(jnp.int32, (8, K), 0)
    lane = lax.broadcasted_iota(jnp.int32, (8, K), 1)
    blocks = K // 8
    g = [gram[i] for i in range(blocks)]
    y = [jnp.where(lane == sub + 8 * i, 1.0, 0.0).astype(F32) for i in range(blocks)]
    for b in range(blocks):
        columns = [lane_copy(g[b], 8 * b + j) for j in range(8)]
        upper, inverse, g_rows, y_rows = {}, [], [], []
        scale = jnp.zeros((8, K), F32)
        for j in range(8):
            pivot = row_copy(columns[j], j)
            inverse.append(1.0 / pivot)
            scale = jnp.where(sub == j, lax.rsqrt(pivot), scale)
            factor = jnp.where(sub > j, columns[j] * inverse[j], 0.0)
            g_rows.append(row_copy(g[b], j))
            y_rows.append(row_copy(y[b], j))
            for m in range(j + 1, 8):
                upper[j, m] = row_copy(columns[m], j)
                columns[m] = columns[m] - factor * upper[j, m]
            g[b] = g[b] - factor * g_rows[j]
            y[b] = y[b] - factor * y_rows[j]
        for i in range(b + 1, blocks):
            factors = []
            gi, yi = g[i], y[i]
            for j in range(8):
                column = lane_copy(g[i], 8 * b + j)
                for m in range(j):
                    column = column - factors[m] * upper[m, j]
                factors.append(column * inverse[j])
                gi = gi - factors[j] * g_rows[j]
                yi = yi - factors[j] * y_rows[j]
            g[i], y[i] = gi, yi
        out_ref[8 * b : 8 * b + 8, :] = y[b] * scale


def kernel(
    a_hbm, s_hbm, proj_out, basis_out,
    a_tile, a_rest, s_all, t_ref, part_wide, part_slim, in_x, in_y, sum_x, sum_y, in_xy,
    in_yx, in_slim, block, z_in, z_all, side_wide, side_slim, gram_part, gram_in, gram_z,
    gram, y_t, y_s, sg_own, sg_in, tp_own, tp_in,
    local_sem, swap_sem, wide_sem, rp_sem, rz_sem, az_sem, ap_sem, gp_sem, gz_sem, ga_sem,
    sg_sem, tp_sem, last_sem, fo_s, fo_r, fo_l,
):
    y = lax.axis_index("grp")
    row = lax.axis_index("row")
    x, z, core = row // (NZ * NC), (row // NC) % NZ, row % NC
    other = 1 - core
    here = x * NY + y

    def at(x_to, y_to, z_to, core_to):
        return (y_to, (x_to * NZ + z_to) * NC + core_to)

    def plane_peer(step):
        x_to, y_to = (x + step[0]) % NX, (y + step[1]) % NY
        return x_to * NY + y_to, at(x_to, y_to, z, core)

    def plane_source(step):
        return (x - step[0]) % NX * NY + (y - step[1]) % NY

    def z_peer(step):
        z_to = (z + step) % NZ
        return z_to, at(x, y, z_to, core)

    partner = at(x, y, z, other)
    plane_peers = [plane_peer(step) for step in PLANE_STEPS]
    z_peers = [z_peer(step) for step in Z_STEPS]
    x_peers = [((x + step) % NX, at((x + step) % NX, y, z, core)) for step in RING]
    y_peers = [((y + step) % NY, at(x, (y + step) % NY, z, core)) for step in RING]

    def send(src, dst, send_sem, recv_sem, device):
        copy = pltpu.make_async_remote_copy(
            src, dst, send_sem, recv_sem, device_id=device, device_id_type=MESH
        )
        copy.start()
        return copy

    def send_all(sem, copies, size):
        for src, dst, device in copies:
            send(src, dst, sem.at[0], sem.at[1], device)
        return pltpu.make_async_remote_copy(
            size, size, sem.at[0], sem.at[1], device_id=partner, device_id_type=MESH
        )

    own_half = pl.ds(pl.multiple_of(core * HALF, HALF), HALF)
    other_half = pl.ds(pl.multiple_of(other * HALF, HALF), HALF)
    loads = [
        pltpu.make_async_copy(a_hbm.at[:, own_half], a_tile.at[core], local_sem.at[0]),
        pltpu.make_async_copy(a_hbm.at[:, other_half], a_rest, local_sem.at[1]),
        pltpu.make_async_copy(s_hbm, s_all, local_sem.at[2]),
    ]
    for copy in loads:
        copy.start()

    barrier = pltpu.get_barrier_semaphore()
    everyone = [device for _, device in plane_peers + z_peers] + [partner]
    for device in everyone:
        pl.semaphore_signal(barrier, inc=1, device_id=device, device_id_type=MESH)
    for copy in loads:
        copy.wait()
    first = jnp.dot(a_tile[core], s_all[own_half, :], preferred_element_type=F32)
    first = first + jnp.dot(a_rest[...], s_all[other_half, :], preferred_element_type=F32)
    t_ref[core] = first.T
    pl.semaphore_wait(barrier, len(everyone))

    swap_t = send(t_ref.at[core], t_ref.at[core], swap_sem.at[0], swap_sem.at[1], partner)
    swap_a = send(a_rest, a_tile.at[core], swap_sem.at[2], swap_sem.at[3], partner)
    swap_t.wait()

    for k in range(STEPS):
        wide, last = k == 0, k == ITERS
        waits = []

        t0, t1 = t_ref[0], t_ref[1]
        local = exact_dot(t0, t0, NT) + exact_dot(t1, t1, NT)
        for i in range(PLANE):
            gram_part[i] = local[8 * i : 8 * i + 8, :]
        gram_wait = send_all(
            gp_sem.at[k],
            [(gram_part.at[q], gram_in.at[k, i], to) for i, (q, to) in enumerate(plane_peers)],
            gram_in.at[k],
        )

        if wide:
            swap_a.wait()
        t0_split = jnp.concatenate(halves(t0), axis=0)
        t1_split = jnp.concatenate(halves(t1), axis=0)
        for j in range(PLANE // 2):
            columns = slice(2 * K * j, 2 * K * (j + 1))
            value = jnp.dot(t0_split, a_tile[0, :, columns], preferred_element_type=F32)
            value = value + jnp.dot(t1_split, a_tile[1, :, columns], preferred_element_type=F32)
            value = value[:K] + value[K:]
            for i in range(2):
                q, part = 2 * j + i, value[:, K * i : K * (i + 1)]
                if wide:
                    part_wide[q // NY, q % NY] = part
                else:
                    part_slim[q] = part.astype(BF16)
        if wide:
            x_wait = send_all(
                wide_sem.at[0],
                [(part_wide.at[q, :, TOP], in_x.at[i], to) for i, (q, to) in enumerate(x_peers)],
                in_x,
            )
            y_wait = send_all(
                wide_sem.at[1],
                [(part_wide.at[:, q, LOW], in_y.at[i], to) for i, (q, to) in enumerate(y_peers)],
                in_y,
            )
            waits += [x_wait, y_wait]
        else:
            into = in_slim.at[k - 1]
            side_wait = send_all(
                rp_sem.at[k],
                [(part_slim.at[q], into.at[i], to) for i, (q, to) in enumerate(plane_peers)],
                into,
            )
            waits += [side_wait]

        gram_wait.wait_recv()
        value = gram_part[here]
        for i in range(PLANE - 1):
            value = value + gram_in[k, i]
        gram_z[k, z] = value
        gram_z_wait = send_all(
            gz_sem.at[k],
            [(gram_z.at[k, z], gram_z.at[k, z], to) for _, to in z_peers],
            gram_z.at[k, pl.ds(0, NZ - 1)],
        )

        if wide:
            x_wait.wait_recv()
            value = part_wide[x, :, TOP]
            for i in range(NX - 1):
                value = value + in_x[i]
            sum_x[...] = value
            xy_wait = send_all(
                wide_sem.at[2],
                [(sum_x.at[q], in_xy.at[i], to) for i, (q, to) in enumerate(y_peers)],
                in_xy,
            )
            y_wait.wait_recv()
            value = part_wide[:, y, LOW]
            for i in range(NY - 1):
                value = value + in_y[i]
            sum_y[...] = value
            yx_wait = send_all(
                wide_sem.at[3],
                [(sum_y.at[q], in_yx.at[i], to) for i, (q, to) in enumerate(x_peers)],
                in_yx,
            )
            xy_wait.wait_recv()
            top = sum_x[y]
            for i in range(NY - 1):
                top = top + in_xy[i]
            yx_wait.wait_recv()
            low = sum_y[x]
            for i in range(NX - 1):
                low = low + in_yx[i]
            value = jnp.concatenate([top, low], axis=0)
            waits += [xy_wait, yx_wait]
        else:
            side_wait.wait_recv()
            value = part_slim[here].astype(F32)
            for i in range(PLANE - 1):
                value = value + into[i].astype(F32)
        for i in range(NZ):
            block[i] = value[PIECE * i : PIECE * (i + 1), :]
        z_wait = send_all(
            rz_sem.at[k],
            [(block.at[q], z_in.at[k, i], to) for i, (q, to) in enumerate(z_peers)],
            z_in.at[k],
        )

        gram_z_wait.wait_recv()
        value = gram_z[k, 0]
        for i in range(1, NZ):
            value = value + gram_z[k, i]
        gram[k, here] = value
        gram_all_wait = send_all(
            ga_sem.at[k],
            [(gram.at[k, here], gram.at[k, here], to) for _, to in plane_peers],
            gram.at[k, pl.ds(0, PLANE - 1)],
        )

        z_wait.wait_recv()
        value = block[z]
        for i in range(NZ - 1):
            value = value + z_in[k, i]
        z_all[k, z] = value
        z_all_wait = send_all(
            az_sem.at[k],
            [(z_all.at[k, z], z_all.at[k, z], to) for _, to in z_peers],
            z_all.at[k, pl.ds(0, NZ - 1)],
        )

        gram_all_wait.wait_recv()
        inverse_factor([gram[k, i] for i in range(PLANE)], y_t)
        y_value = y_t[...]

        z_all_wait.wait_recv()
        value = z_all[k].reshape(K, K)
        waits += [gram_wait, gram_z_wait, z_wait, gram_all_wait, z_all_wait]
        if wide:
            side_wide[x, y] = exact_dot(y_value, value)
            x_wait = send_all(
                wide_sem.at[4],
                [(side_wide.at[x, y, TOP], side_wide.at[x, y, TOP], to) for _, to in x_peers],
                side_wide.at[0, pl.ds(0, NX - 1), TOP],
            )
            y_wait = send_all(
                wide_sem.at[5],
                [(side_wide.at[x, y, LOW], side_wide.at[x, y, LOW], to) for _, to in y_peers],
                side_wide.at[0, pl.ds(0, NY - 1), LOW],
            )
            x_wait.wait_recv()
            xy_wait = send_all(
                wide_sem.at[6],
                [(side_wide.at[:, y, TOP], side_wide.at[:, y, TOP], to) for _, to in y_peers],
                side_wide.at[pl.ds(0, NY - 1), :, TOP],
            )
            y_wait.wait_recv()
            yx_wait = send_all(
                wide_sem.at[7],
                [(side_wide.at[x, :, LOW], side_wide.at[x, :, LOW], to) for _, to in x_peers],
                side_wide.at[pl.ds(0, NX - 1), :, LOW],
            )
            xy_wait.wait_recv()
            yx_wait.wait_recv()
            waits += [x_wait, y_wait, xy_wait, yx_wait]
        elif not last:
            whole = side_slim.at[k - 1]
            whole[here] = exact_dot(y_value, value).astype(BF16)
            all_wait = send_all(
                ap_sem.at[k],
                [(whole.at[here], whole.at[here], to) for _, to in plane_peers],
                whole.at[pl.ds(0, PLANE - 1)],
            )
            all_wait.wait_recv()
            waits += [all_wait]
        else:
            whole = side_slim.at[k - 1]
            whole[here] = exact_dot(value, y_value / SCALE, TN).astype(BF16)
            copies = [
                send(whole.at[here], whole.at[here], last_sem.at[0, i], last_sem.at[1, i], to)
                for i, (_, to) in enumerate(plane_peers)
            ]

            def pass_on(i, q):
                keep = pltpu.make_async_copy(whole.at[q], proj_out.at[core, q], fo_l.at[i])
                keep.start()
                to = proj_out.at[core, q]
                return [keep, send(whole.at[q], to, fo_s.at[i], fo_r.at[i], partner)]

            outs = pass_on(PLANE - 1, here)
            basis_out[...] = exact_dot(t_ref[core], y_value * SCALE, TN)
            for i in reversed(range(PLANE - 1)):
                copies[i].wait_recv()
                outs += pass_on(i, plane_source(PLANE_STEPS[i]))
            for copy in copies:
                copy.wait_send()
            for copy in outs:
                copy.wait()
        for wait in waits:
            wait.wait_send()
        if last:
            break

        pairs = []
        for j in range(PLANE // 2):
            if wide:
                p, q = j // 2, 2 * (j % 2)
                pair = jnp.concatenate([side_wide[p, q], side_wide[p, q + 1]], axis=1)
                pairs.append(jnp.concatenate(halves(pair), axis=0))
            else:
                pairs.append(jnp.concatenate([whole[2 * j], whole[2 * j + 1]], axis=1))
        split = jnp.concatenate(pairs, axis=1)
        total = lax.dot_general(split, split, NT, preferred_element_type=F32)
        if wide:
            total = total[:K] + total[K:]
            total = total[:, :K] + total[:, K:]
        sg_own[...] = total
        swap_gram = send(sg_own, sg_in.at[k], sg_sem.at[k, 0], sg_sem.at[k, 1], partner)
        for half in range(NC):
            value = lax.dot_general(split, a_tile[half], NT, preferred_element_type=F32)
            tp_own[half] = value[:K] + value[K:] if wide else value
        swap_part = send(tp_own, tp_in.at[k], tp_sem.at[k, 0], tp_sem.at[k, 1], partner)
        swap_gram.wait()
        total = sg_own[...] + sg_in[k]
        inverse_factor([total[8 * i : 8 * i + 8, :] for i in range(PLANE)], y_s)
        swap_part.wait()
        y_value = y_s[...]
        for half in range(NC):
            t_ref[half] = exact_dot(y_value, tp_own[half] + tp_in[k, half])


def sweep(embeddings, sketch):
    vmem = pl.BlockSpec(memory_space=pltpu.VMEM)
    hbm = pl.BlockSpec(memory_space=pl.ANY)
    dma = pltpu.SemaphoreType.DMA
    near, far = PLANE - 1, NZ - 1
    return pl.pallas_call(
        kernel,
        out_shape=(
            jax.ShapeDtypeStruct((NC, PLANE, K, K), BF16),
            jax.ShapeDtypeStruct((ROWS, K), F32),
        ),
        in_specs=[hbm, hbm],
        out_specs=(hbm, vmem),
        scratch_shapes=[
            pltpu.VMEM((NC, ROWS, HALF), BF16),
            pltpu.VMEM((ROWS, HALF), BF16),
            pltpu.VMEM((D, K), BF16),
            pltpu.VMEM((NC, K, ROWS), F32),
            pltpu.VMEM((NX, NY, K, K), F32),
            pltpu.VMEM((PLANE, K, K), BF16),
            pltpu.VMEM((NX - 1, NY, K // 2, K), F32),
            pltpu.VMEM((NY - 1, NX, K // 2, K), F32),
            pltpu.VMEM((NY, K // 2, K), F32),
            pltpu.VMEM((NX, K // 2, K), F32),
            pltpu.VMEM((NY - 1, K // 2, K), F32),
            pltpu.VMEM((NX - 1, K // 2, K), F32),
            pltpu.VMEM((ITERS, near, K, K), BF16),
            pltpu.VMEM((NZ, PIECE, K), F32),
            pltpu.VMEM((STEPS, far, PIECE, K), F32),
            pltpu.VMEM((STEPS, NZ, PIECE, K), F32),
            pltpu.VMEM((NX, NY, K, K), F32),
            pltpu.VMEM((ITERS, PLANE, K, K), BF16),
            pltpu.VMEM((PLANE, 8, K), F32),
            pltpu.VMEM((STEPS, near, 8, K), F32),
            pltpu.VMEM((STEPS, NZ, 8, K), F32),
            pltpu.VMEM((STEPS, PLANE, 8, K), F32),
            pltpu.VMEM((K, K), F32),
            pltpu.VMEM((K, K), F32),
            pltpu.VMEM((K, K), F32),
            pltpu.VMEM((ITERS, K, K), F32),
            pltpu.VMEM((NC, K, ROWS), F32),
            pltpu.VMEM((ITERS, NC, K, ROWS), F32),
            dma((3,)), dma((4,)), dma((8, 2)),
            dma((STEPS, 2)), dma((STEPS, 2)), dma((STEPS, 2)), dma((STEPS, 2)),
            dma((STEPS, 2)), dma((STEPS, 2)), dma((STEPS, 2)),
            dma((ITERS, 2)), dma((ITERS, 2)),
            dma((2, near)), dma((PLANE,)), dma((PLANE,)), dma((PLANE,)),
        ],
        compiler_params=pltpu.CompilerParams(
            collective_id=0, has_side_effects=True, vmem_limit_bytes=62 * 2**20
        ),
        name="sweep",
    )(embeddings, sketch)


def finish_kernel(proj_ref, basis_ref, basis_out, proj_out):
    proj_out[...] = proj_ref[...].astype(F32)
    basis_out[...] = basis_ref[...]


def finish(projected, basis):
    steps = 4
    tall = pl.BlockSpec((D // steps, K), lambda i: (i, 0))
    short = pl.BlockSpec((ROWS // steps, K), lambda i: (i, 0))
    return pl.pallas_call(
        finish_kernel,
        grid=(steps,),
        out_shape=(
            jax.ShapeDtypeStruct((ROWS, K), F32),
            jax.ShapeDtypeStruct((D, K), F32),
        ),
        in_specs=[tall, short],
        out_specs=(short, tall),
        name="finish",
    )(projected, basis)


def per_device(embeddings, sketch):
    projected, basis = sweep(embeddings, sketch)
    return finish(projected.reshape(D, K), basis)


def solution(mesh):
    return jax.shard_map(
        per_device,
        mesh=mesh,
        in_specs=(P(("grp", "row"), None), P()),
        out_specs=(P(("grp", "row"), None), P()),
        check_vma=False,
    )
```

time: 134 us -> 119 us (0.89)
  Pallas kernels: 130 us -> 119 us
  other arithmetic: 2.71 us -> 0 us
    pallas_call x1, Pallas kernels: 130 us -> 115 us  [sweep(): pl.pallas_call(kernel, out_shape=(jax.ShapeDtypeStruct((NC, PLANE, K, K),...]
    pallas_call x0 -> x1, Pallas kernels: none -> 3.6 us  [finish(): pl.pallas_call(finish_kernel, grid=(steps,), out_shape=(jax.ShapeDtypeStr...]
    convert_element_type x1 -> x0, other arithmetic: 2.71 us -> none  [per_device(): return (basis, projected.reshape(D, K).astype(F32))]
where the time goes in v3:
time: 119 us
  Pallas kernels  119 us (100%)
    pallas_call x1, Pallas kernels, sweep(): pl.pallas_call(kernel, out_shape=(jax.ShapeDtypeStruct((NC, PLANE, K, K),...  115 us
    pallas_call x1, Pallas kernels, finish(): pl.pallas_call(finish_kernel, grid=(steps,), out_shape=(jax.ShapeDtypeStr...  3.6 us

profile of v3, /device:TPU:1, one launch (start us, length us, event | category | flops | bytes accessed | tf_op | source)
XLA Modules:
  0.0 119.3 jit_solution(16962300375703410519)
XLA Ops:
  0.6 115.0 %sweep.1 = (bf16[2,16,128,128]{3,2,1,0:T(8,128)(2,1)}, f32[256,128]{1,0:T(8,128)}) custom-call(bf16[256,4096]{1,0:T(8,128)(2,1)} %a_hbm.1, bf16[4096,128]{1,0:T(8,128)(2,1)} %s_hbm.1), custom_call_target="tpu_custom_call" | custom-call | tf_op jit(solution)/shard_map/sweep/pallas_call | solution.py:402
  115.7 3.6 %finish.1 = (f32[256,128]{1,0:T(8,128)}, f32[4096,128]{1,0:T(8,128)}) custom-call(bf16[4096,128]{1,0:T(8,128)(2,1)} %bitcast.1, f32[256,128]{1,0:T(8,128)} %get-tuple-element.5.basis_ref), custom_call_target="tpu_custom_call" | custom-call | tf_op jit(solution)/shard_map/finish/pallas_call | solution.py:461

commit v4 on v3

--- a/solution.py
+++ b/solution.py
@@ -27,10 +27,7 @@
 
 RING = [2, 1, 3]
 Z_STEPS = sorted(range(1, NZ), key=lambda c: -hops(c, NZ))
-PLANE_STEPS = sorted(
-    [(a, b) for a in range(NX) for b in range(NY) if (a, b) != (0, 0)],
-    key=lambda c: -hops(c[0], NX) - hops(c[1], NY),
-)
+PLANE_STEPS = [(a, b) for a in RING + [0] for b in RING + [0] if (a, b) != (0, 0)]
 SCALE = math.sqrt(ROWS * NX * NY * NZ * NC)
 NT = (((1,), (1,)), ((), ()))
 TN = (((0,), (1,)), ((), ()))
@@ -62,24 +59,43 @@
     sub = lax.broadcasted_iota(jnp.int32, (8, K), 0)
     lane = lax.broadcasted_iota(jnp.int32, (8, K), 1)
     blocks = K // 8
-    g = [gram[i] for i in range(blocks)]
-    y = [jnp.where(lane == sub + 8 * i, 1.0, 0.0).astype(F32) for i in range(blocks)]
+    diagonal = [jnp.where(lane == sub + 8 * i, gram[i], 0.0) for i in range(blocks)]
+    total = diagonal[0]
+    for i in range(1, blocks):
+        total = total + diagonal[i]
+    lanes = jnp.broadcast_to(lax.rsqrt(jnp.sum(total, axis=0, keepdims=True)), (8, K))
+    y = [jnp.where(lane == sub + 8 * i, lanes, 0.0) for i in range(blocks)]
+    g = [
+        gram[i] * lanes * lax.rsqrt(jnp.sum(diagonal[i], axis=1, keepdims=True))
+        for i in range(blocks)
+    ]
     for b in range(blocks):
         columns = [lane_copy(g[b], 8 * b + j) for j in range(8)]
         upper, inverse, g_rows, y_rows = {}, [], [], []
         scale = jnp.zeros((8, K), F32)
-        for j in range(8):
-            pivot = row_copy(columns[j], j)
-            inverse.append(1.0 / pivot)
-            scale = jnp.where(sub == j, lax.rsqrt(pivot), scale)
-            factor = jnp.where(sub > j, columns[j] * inverse[j], 0.0)
+        for j in range(0, 8, 2):
+            first, cross = row_copy(columns[j], j), row_copy(columns[j + 1], j)
+            second = row_copy(columns[j + 1], j + 1)
+            minor = first * second - cross * cross
+            inverse += [1.0 / first, first * (1.0 / minor)]
+            upper[j, j + 1] = cross
+            scale = jnp.where(sub == j, lax.rsqrt(first), scale)
+            scale = jnp.where(sub == j + 1, lax.rsqrt(minor * inverse[j]), scale)
+            f0 = jnp.where(sub > j, columns[j], 0.0) * inverse[j]
+            f1 = jnp.where(sub > j + 1, columns[j + 1] - f0 * cross, 0.0) * inverse[j + 1]
             g_rows.append(row_copy(g[b], j))
             y_rows.append(row_copy(y[b], j))
-            for m in range(j + 1, 8):
+            g_next = g[b] - f0 * g_rows[j]
+            y_next = y[b] - f0 * y_rows[j]
+            g_rows.append(row_copy(g_next, j + 1))
+            y_rows.append(row_copy(y_next, j + 1))
+            g[b] = g_next - f1 * g_rows[j + 1]
+            y[b] = y_next - f1 * y_rows[j + 1]
+            for m in range(j + 2, 8):
                 upper[j, m] = row_copy(columns[m], j)
-                columns[m] = columns[m] - factor * upper[j, m]
-            g[b] = g[b] - factor * g_rows[j]
-            y[b] = y[b] - factor * y_rows[j]
+                column = columns[m] - f0 * upper[j, m]
+                upper[j + 1, m] = row_copy(column, j + 1)
+                columns[m] = column - f1 * upper[j + 1, m]
         for i in range(b + 1, blocks):
             factors = []
             gi, yi = g[i], y[i]
@@ -361,9 +377,9 @@
                 copy.wait_send()
             for copy in outs:
                 copy.wait()
-        for wait in waits:
-            wait.wait_send()
         if last:
+            for wait in waits:
+                wait.wait_send()
             break
 
         pairs = []
@@ -392,6 +408,8 @@
         y_value = y_s[...]
         for half in range(NC):
             t_ref[half] = exact_dot(y_value, tp_own[half] + tp_in[k, half])
+        for wait in waits:
+            wait.wait_send()
 
 
 def sweep(embeddings, sketch):
@@ -455,7 +473,7 @@
 
 
 def finish(projected, basis):
-    steps = 4
+    steps = 2
     tall = pl.BlockSpec((D // steps, K), lambda i: (i, 0))
     short = pl.BlockSpec((ROWS // steps, K), lambda i: (i, 0))
     return pl.pallas_call(

time: 119 us -> 117 us (0.983)
  Pallas kernels: 119 us -> 117 us
where the time goes in v4:
time: 117 us
  Pallas kernels  117 us (100%)
    pallas_call x1, Pallas kernels, sweep(): pl.pallas_call(kernel, out_shape=(jax.ShapeDtypeStruct((NC, PLANE, K, K),...  114 us
    pallas_call x1, Pallas kernels, finish(): pl.pallas_call(finish_kernel, grid=(steps,), out_shape=(jax.ShapeDtypeStr...  2.47 us

profile of v4, /device:TPU:1, one launch (start us, length us, event | category | flops | bytes accessed | tf_op | source)
XLA Modules:
  0.0 117.3 jit_solution(4799887459646461632)
XLA Ops:
  0.6 114.1 %sweep.1 = (bf16[2,16,128,128]{3,2,1,0:T(8,128)(2,1)}, f32[256,128]{1,0:T(8,128)}) custom-call(bf16[256,4096]{1,0:T(8,128)(2,1)} %a_hbm.1, bf16[4096,128]{1,0:T(8,128)(2,1)} %s_hbm.1), custom_call_target="tpu_custom_call" | custom-call | tf_op jit(solution)/shard_map/sweep/pallas_call | solution.py:420
  114.8 2.5 %finish.1 = (f32[256,128]{1,0:T(8,128)}, f32[4096,128]{1,0:T(8,128)}) custom-call(bf16[4096,128]{1,0:T(8,128)(2,1)} %bitcast.1, f32[256,128]{1,0:T(8,128)} %get-tuple-element.5.basis_ref), custom_call_target="tpu_custom_call" | custom-call | tf_op jit(solution)/shard_map/finish/pallas_call | solution.py:479

commit v5 on v4

--- a/solution.py
+++ b/solution.py
@@ -165,13 +165,12 @@
         pltpu.make_async_copy(a_hbm.at[:, other_half], a_rest, local_sem.at[1]),
         pltpu.make_async_copy(s_hbm, s_all, local_sem.at[2]),
     ]
-    for copy in loads:
-        copy.start()
-
     barrier = pltpu.get_barrier_semaphore()
     everyone = [device for _, device in plane_peers + z_peers] + [partner]
     for device in everyone:
         pl.semaphore_signal(barrier, inc=1, device_id=device, device_id_type=MESH)
+    for copy in loads:
+        copy.start()
     for copy in loads:
         copy.wait()
     first = jnp.dot(a_tile[core], s_all[own_half, :], preferred_element_type=F32)
@@ -198,20 +197,35 @@
         )
 
         if wide:
+            mine = jnp.concatenate(halves(t_ref[core]), axis=0)
+            theirs = jnp.concatenate(halves(t_ref[other]), axis=0)
+            for j in range(PLANE // 2):
+                columns = slice(2 * K * j, 2 * K * (j + 1))
+                value = jnp.dot(mine, a_tile[core, :, columns], preferred_element_type=F32)
+                value = value[:K] + value[K:]
+                for i in range(2):
+                    q = 2 * j + i
+                    part_wide[q // NY, q % NY] = value[:, K * i : K * (i + 1)]
             swap_a.wait()
-        t0_split = jnp.concatenate(halves(t0), axis=0)
-        t1_split = jnp.concatenate(halves(t1), axis=0)
-        for j in range(PLANE // 2):
-            columns = slice(2 * K * j, 2 * K * (j + 1))
-            value = jnp.dot(t0_split, a_tile[0, :, columns], preferred_element_type=F32)
-            value = value + jnp.dot(t1_split, a_tile[1, :, columns], preferred_element_type=F32)
-            value = value[:K] + value[K:]
-            for i in range(2):
-                q, part = 2 * j + i, value[:, K * i : K * (i + 1)]
-                if wide:
-                    part_wide[q // NY, q % NY] = part
-                else:
-                    part_slim[q] = part.astype(BF16)
+            for j in range(PLANE // 2):
+                columns = slice(2 * K * j, 2 * K * (j + 1))
+                value = jnp.dot(theirs, a_tile[other, :, columns], preferred_element_type=F32)
+                value = value[:K] + value[K:]
+                for i in range(2):
+                    q = 2 * j + i
+                    part_wide[q // NY, q % NY] += value[:, K * i : K * (i + 1)]
+        else:
+            t0_split = jnp.concatenate(halves(t0), axis=0)
+            t1_split = jnp.concatenate(halves(t1), axis=0)
+            for j in range(PLANE // 2):
+                columns = slice(2 * K * j, 2 * K * (j + 1))
+                value = jnp.dot(t0_split, a_tile[0, :, columns], preferred_element_type=F32)
+                value = value + jnp.dot(
+                    t1_split, a_tile[1, :, columns], preferred_element_type=F32
+                )
+                value = value[:K] + value[K:]
+                for i in range(2):
+                    part_slim[2 * j + i] = value[:, K * i : K * (i + 1)].astype(BF16)
         if wide:
             x_wait = send_all(
                 wide_sem.at[0],

time: 117 us -> 117 us (level)
  no operation moved by 1% of the time
where the time goes in v5:
time: 117 us
  Pallas kernels  116 us (99%)
    pallas_call x1, Pallas kernels, sweep(): pl.pallas_call(kernel, out_shape=(jax.ShapeDtypeStruct((NC, PLANE, K, K),...  113 us
    pallas_call x1, Pallas kernels, finish(): pl.pallas_call(finish_kernel, grid=(steps,), out_shape=(jax.ShapeDtypeStr...  2.47 us

profile of v5, /device:TPU:1, one launch (start us, length us, event | category | flops | bytes accessed | tf_op | source)
XLA Modules:
  0.0 116.6 jit_solution(13226832254017284439)
XLA Ops:
  0.6 113.5 %sweep.1 = (bf16[2,16,128,128]{3,2,1,0:T(8,128)(2,1)}, f32[256,128]{1,0:T(8,128)}) custom-call(bf16[256,4096]{1,0:T(8,128)(2,1)} %a_hbm.1, bf16[4096,128]{1,0:T(8,128)(2,1)} %s_hbm.1), custom_call_target="tpu_custom_call" | custom-call | tf_op jit(solution)/shard_map/sweep/pallas_call | solution.py:434
  114.1 2.5 %finish.1 = (f32[256,128]{1,0:T(8,128)}, f32[4096,128]{1,0:T(8,128)}) custom-call(bf16[4096,128]{1,0:T(8,128)(2,1)} %bitcast.1, f32[256,128]{1,0:T(8,128)} %get-tuple-element.5.basis_ref), custom_call_target="tpu_custom_call" | custom-call | tf_op jit(solution)/shard_map/finish/pallas_call | solution.py:493
